TPU v7x, 256 devices: a whole 4x4x8 slice. The times are simulated.
256 devices in a mesh: feat: 64 (over x, z_lo, y), dp: 4 (over z_hi, core).
Axes of the slice: x: 4, y: 4, z: 8 (z_hi: 2, z_lo: 4; z = z_hi * 4 + z_lo), core: 2. Of those that a mesh axis runs over, the one named last changes fastest.
Arguments:
- inputs: bfloat16 [1024, 65536], P('dp', 'feat'), may hold values from -6 to 6
- weights: bfloat16 [128, 8, 512, 512], P('feat'), may hold values from -0.09375 to 0.09375
- cotangent: bfloat16 [1024, 65536], P('dp', 'feat'), may hold values from -0.75 to 0.75
Outputs:
- outputs: bfloat16 [1024, 65536], P('dp', 'feat')
- input_grad: bfloat16 [1024, 65536], P('dp', 'feat')
- weight_grad: bfloat16 [128, 8, 512, 512], P('feat', None, 'dp')
All inputs are finite; a program needn't handle non-finite values.
Results may differ from a plain program's by a relative error of at most 0.0047.
Values may be sent and summed in bfloat16 or wider, within the bound.
A program may use at most 128 MiB of HBM per device.

v0:
```python
import jax
import jax.numpy as jnp
from jax import lax
from jax.sharding import PartitionSpec as P


def partner(value, axis, distance):
    mask = 2**distance
    pairs = [(source, source ^ mask) for source in range(lax.axis_size(axis))]
    return lax.ppermute(value, axis, pairs)


def flip_rows(values, bit_level):
    row_count, tokens, last_size = values.shape
    halves = values.reshape(row_count >> bit_level + 1, 2, 1 << bit_level, tokens, last_size)
    return jnp.flip(halves, 1).reshape(row_count, tokens, last_size)


def body(inputs, weights, cotangent):
    row_count = weights.shape[0]
    slot_count = weights.shape[1]
    block_size = weights.shape[2]
    levels = slot_count - 1
    tokens = inputs.shape[0]
    local_bits = row_count.bit_length() - 1
    features = jnp.transpose(inputs.reshape(tokens, row_count, block_size), (1, 0, 2))
    upstream = jnp.transpose(cotangent.reshape(tokens, row_count, block_size), (1, 0, 2))
    visit_list = list(range(levels))
    partner_rows = {}
    for bit_level in visit_list:
        if bit_level < local_bits:
            partner_rows[bit_level] = flip_rows(features, bit_level)
        else:
            partner_rows[bit_level] = partner(features, "feat", bit_level - local_bits)
    forward_stack = jnp.stack([features] + [partner_rows[level] for level in range(levels)], axis=1)
    summed = jnp.einsum(
        "rsta,rsab->rtb", forward_stack, weights, preferred_element_type=jnp.float32
    )
    outputs = jnp.transpose(summed.astype(jnp.bfloat16), (1, 0, 2)).reshape(
        tokens, row_count * block_size
    )
    back_terms = jnp.einsum("rtb,rsab->rsta", upstream, weights, preferred_element_type=jnp.float32)
    grad_total = back_terms[:, 0]
    rounded_terms = back_terms[:, 1:].astype(jnp.bfloat16)
    for bit_level in range(levels):
        partial_term = rounded_terms[:, bit_level]
        if bit_level < local_bits:
            arrived = flip_rows(partial_term, bit_level)
        else:
            arrived = partner(partial_term, "feat", bit_level - local_bits)
        grad_total = grad_total + arrived.astype(jnp.float32)
    input_grad = jnp.transpose(grad_total.astype(jnp.bfloat16), (1, 0, 2)).reshape(
        tokens, row_count * block_size
    )
    columns = lax.all_to_all(forward_stack, "dp", split_axis=3, concat_axis=2, tiled=True)
    weight_sum = jnp.einsum(
        "rsta,rtb->rsab",
        columns,
        lax.all_gather(upstream, "dp", axis=1, tiled=True),
        preferred_element_type=jnp.float32,
    )
    weight_grad = weight_sum.astype(jnp.bfloat16)
    return (outputs, input_grad, weight_grad)


def solution(mesh):
    in_specs = (P("dp", "feat"), P("feat", None, None, None), P("dp", "feat"))
    out_specs = (P("dp", "feat"), P("dp", "feat"), P("feat", None, "dp", None))
    return jax.shard_map(body, mesh=mesh, in_specs=in_specs, out_specs=out_specs, check_vma=False)
```

profile of v0, /device:TPU:3, one launch (start us, length us, event | category | flops | bytes accessed | tf_op | source)
XLA Modules:
  0.0 235.9 jit_solution(11875098161094299809)
XLA Ops:
  7.2 1.2 copy.44
  8.4 0.2 copy.45
  8.6 1.4 collective-permute-start
  10.0 2.6 %collective-permute-start.1 = (bf16[2,256,512]{2,1,0:T(8,128)(2,1)S(1)}, bf16[2,256,512]{2,1,0:T(8,128)(2,1)S(1)}, u32[]{:S(2)}, u32[]{:S(2)}) collective-permute-start(bf16[2,256,512]{2,1,0:T(8,128)(2,1)S(1)} %bitcast.137), channel_id=1, source_target_pairs={{0,8},{4,12},{8,0},{12,4},{16,24},{20,28},{24,16},{28,20},{32,40},... | collective-permute-start | bytes 1572872 | tf_op jit(solution)/shard_map/ppermute | solution.py:10
  12.6 1.6 collective-permute-start.2
  14.3 3.0 %collective-permute-start.3 = (bf16[2,256,512]{2,1,0:T(8,128)(2,1)S(1)}, bf16[2,256,512]{2,1,0:T(8,128)(2,1)S(1)}, u32[]{:S(2)}, u32[]{:S(2)}) collective-permute-start(bf16[2,256,512]{2,1,0:T(8,128)(2,1)S(1)} %bitcast.139), channel_id=1, source_target_pairs={{0,32},{4,36},{8,40},{12,44},{16,48},{20,52},{24,56},{28,60},{32,0... | collective-permute-start | bytes 1572872 | tf_op jit(solution)/shard_map/ppermute | solution.py:10
  17.3 0.3 collective-permute-start.4
  17.5 0.8 bitcast_dynamic-update-slice_fusion.6
  18.4 0.9 bitcast_dynamic-update-slice_fusion.5
  19.2 2.3 collective-permute-done
  21.5 1.8 collective-permute-start.5
  23.4 0.9 bitcast_dynamic-update-slice_fusion.4
  24.2 11.0 %collective-permute-done.1 = bf16[2,256,512]{2,1,0:T(8,128)(2,1)S(1)} collective-permute-done((bf16[2,256,512]{2,1,0:T(8,128)(2,1)S(1)}, bf16[2,256,512]{2,1,0:T(8,128)(2,1)S(1)}, u32[]{:S(2)}, u32[]{:S(2)}) %collective-permute-start.1) | collective-permute-done | bytes 524320 | tf_op jit(solution)/shard_map/ppermute | solution.py:10
  35.2 0.8 bitcast_dynamic-update-slice_fusion.3
  36.0 0.1 collective-permute-done.2
  36.2 0.8 bitcast_dynamic-update-slice_fusion.2
  37.0 0.0 collective-permute-done.3
  37.0 0.8 bitcast_dynamic-update-slice_fusion.1
  37.8 0.0 collective-permute-done.4
  37.8 0.8 bitcast_dynamic-update-slice_fusion
  38.6 2.4 %collective-permute-done.5 = bf16[2,256,512]{2,1,0:T(8,128)(2,1)S(1)} collective-permute-done((bf16[2,256,512]{2,1,0:T(8,128)(2,1)S(1)}, bf16[2,256,512]{2,1,0:T(8,128)(2,1)S(1)}, u32[]{:S(2)}, u32[]{:S(2)}) %collective-permute-start.5) | collective-permute-done | bytes 524320 | tf_op jit(solution)/shard_map/ppermute | solution.py:10
  41.0 0.8 bitcast_dynamic-update-slice_fusion.7
  41.9 7.9 %copy.63 = bf16[2,8,256,512]{2,1,0,3:T(8,128)(2,1)} copy(bf16[2,8,256,512]{3,2,1,0:T(8,128)(2,1)} %bitcast_dynamic-update-slice_fusion.7) | data formatting | bytes 8388608 | tf_op jit(solution)/shard_map/stack | solution.py:35
  49.8 9.1 %all-to-all-start = ((bf16[2,8,256,512]{2,1,0,3:T(8,128)(2,1)}), bf16[2,8,256,512]{2,1,0,3:T(8,128)(2,1)}, u32[]{:S(2)}, u32[]{:S(2)}) async-start(bf16[2,8,256,512]{2,1,0,3:T(8,128)(2,1)} %copy.63), calls=%async_computation | async-start | bytes 8388608 | tf_op jit(solution)/shard_map/all_to_all | solution.py:55
  58.9 0.2 copy.54
  59.1 1.0 copy.55
  60.1 0.0 all-gather.2.cloned.1.call-update
  60.1 5.8 %fusion.17 = (bf16[2,8,256,512]{2,3,1,0:T(8,128)(2,1)S(1)}, f32[2,8,256,512]{2,3,1,0:T(8,128)S(1)}) fusion(bf16[2,8,512,512]{3,2,1,0:T(8,128)(2,1)} %param.4, bf16[256,2,512]{2,0,1:T(8,128)(2,1)} %copy.55), kind=kOutput, calls=%fused_computation.34 | convolution fusion | flops 2149580800 | bytes 21495808 | tf_op jit(solution)/shard_map/rtb,rsab->rsta/dot_general | solution.py:42
  65.9 0.3 slice_bitcast_fusion.7
  66.2 1.1 collective-permute-start.10
  67.4 1.3 collective-permute-start.11
  68.7 0.0 collective-permute-start.6
  68.7 1.1 collective-permute-start.7
  69.8 10.1 %collective-permute-done.10 = bf16[2,256,512]{1,2,0:T(8,128)(2,1)S(1)} collective-permute-done((bf16[2,256,512]{1,2,0:T(8,128)(2,1)S(1)}, bf16[2,256,512]{1,2,0:T(8,128)(2,1)S(1)}, u32[]{:S(2)}, u32[]{:S(2)}) %collective-permute-start.10) | collective-permute-done | bytes 524320 | tf_op jit(solution)/shard_map/ppermute | solution.py:10
  80.0 0.8 collective-permute-start.9
  80.8 11.3 %collective-permute-done.11 = bf16[2,256,512]{1,2,0:T(8,128)(2,1)S(1)} collective-permute-done((bf16[2,256,512]{1,2,0:T(8,128)(2,1)S(1)}, bf16[2,256,512]{1,2,0:T(8,128)(2,1)S(1)}, u32[]{:S(2)}, u32[]{:S(2)}) %collective-permute-start.11) | collective-permute-done | bytes 524320 | tf_op jit(solution)/shard_map/ppermute | solution.py:10
  92.1 0.5 collective-permute-done.7
  92.6 102.6 %collective-permute-done.8 = bf16[2,256,512]{1,2,0:T(8,128)(2,1)S(1)} collective-permute-done((bf16[2,256,512]{1,2,0:T(8,128)(2,1)S(1)}, bf16[2,256,512]{1,2,0:T(8,128)(2,1)S(1)}, u32[]{:S(2)}, u32[]{:S(2)}) %collective-permute-start.8) | collective-permute-done | bytes 524320 | tf_op jit(solution)/shard_map/ppermute | solution.py:10
  195.2 2.4 %collective-permute-done.9 = bf16[2,256,512]{1,2,0:T(8,128)(2,1)S(1)} collective-permute-done((bf16[2,256,512]{1,2,0:T(8,128)(2,1)S(1)}, bf16[2,256,512]{1,2,0:T(8,128)(2,1)S(1)}, u32[]{:S(2)}, u32[]{:S(2)}) %collective-permute-start.9) | collective-permute-done | bytes 524320 | tf_op jit(solution)/shard_map/ppermute | solution.py:10
  197.6 0.6 fusion.15
  198.2 1.0 copy.66
  199.2 7.0 %fusion.6 = bf16[256,2,512]{2,0,1:T(8,128)(2,1)S(1)} fusion(bf16[2,8,256,512]{3,2,1,0:T(8,128)(2,1)} %bitcast_dynamic-update-slice_fusion.7, bf16[2,8,512,512]{3,2,1,0:T(8,128)(2,1)} %param.4), kind=kOutput, calls=%fused_computation.7 | convolution fusion | flops 2147745792 | bytes 13107200 | tf_op jit(solution)/shard_map/rsta,rsab->rtb/dot_general | solution.py:36
  206.2 0.2 copy.53
  206.4 1.0 copy.65
  207.4 0.0 all-to-all-done
  207.4 7.4 %copy.78 = bf16[2,8,256,4,128]{2,3,4,1,0:T(4,128)(2,1)} copy(bf16[2,8,256,4,128]{2,1,0,4,3:T(8,128)(2,1)} %bitcast.35) | data formatting | bytes 8388608 | tf_op jit(solution)/shard_map/all_to_all | solution.py:55
  214.8 7.7 %all_to_all.16 = bf16[2,8,1024,128]{2,3,1,0:T(8,128)(2,1)} reshape(bf16[2,8,4,256,128]{3,2,4,1,0:T(4,128)(2,1)} %bitcast.135) | data formatting | bytes 8388608 | tf_op jit(solution)/shard_map/all_to_all | solution.py:55
  222.5 6.5 %fusion.2 = bf16[2,8,128,512]{3,2,1,0:T(8,128)(2,1)} fusion(bf16[2,8,1024,128]{2,3,1,0:T(8,128)(2,1)} %all_to_all.16, bf16[2,1024,512]{2,1,0:T(8,128)(2,1)} %all-gather.2.cloned.1.call-done), kind=kOutput, calls=%fused_computation.4 | convolution fusion | flops 2148532224 | bytes 8388608 | tf_op jit(solution)/shard_map/rsta,rtb->rsab/dot_general | solution.py:56
  (6 shorter events, 0.0 us)
Async XLA Ops:
  8.6 12.9 %collective-permute-start = (bf16[2,256,512]{2,1,0:T(8,128)(2,1)S(1)}, bf16[2,256,512]{2,1,0:T(8,128)(2,1)S(1)}, u32[]{:S(2)}, u32[]{:S(2)}) collective-permute-start(bf16[2,256,512]{2,1,0:T(8,128)(2,1)S(1)} %bitcast.136), channel_id=1, source_target_pairs={{0,4},{4,0},{8,12},{12,8},{16,20},{20,16},{24,28},{28,24},{32,36},... | collective-permute-start | bytes 1572872 | tf_op jit(solution)/shard_map/ppermute | solution.py:10
  10.0 25.2 %collective-permute-start.1 = (bf16[2,256,512]{2,1,0:T(8,128)(2,1)S(1)}, bf16[2,256,512]{2,1,0:T(8,128)(2,1)S(1)}, u32[]{:S(2)}, u32[]{:S(2)}) collective-permute-start(bf16[2,256,512]{2,1,0:T(8,128)(2,1)S(1)} %bitcast.137), channel_id=1, source_target_pairs={{0,8},{4,12},{8,0},{12,4},{16,24},{20,28},{24,16},{28,20},{32,40},... | collective-permute-start | bytes 1572872 | tf_op jit(solution)/shard_map/ppermute | solution.py:10
  12.6 23.5 %collective-permute-start.2 = (bf16[2,256,512]{2,1,0:T(8,128)(2,1)S(1)}, bf16[2,256,512]{2,1,0:T(8,128)(2,1)S(1)}, u32[]{:S(2)}, u32[]{:S(2)}) collective-permute-start(bf16[2,256,512]{2,1,0:T(8,128)(2,1)S(1)} %bitcast.138), channel_id=1, source_target_pairs={{0,16},{4,20},{8,24},{12,28},{16,0},{20,4},{24,8},{28,12},{32,48},... | collective-permute-start | bytes 1572872 | tf_op jit(solution)/shard_map/ppermute | solution.py:10
  14.3 22.7 %collective-permute-start.3 = (bf16[2,256,512]{2,1,0:T(8,128)(2,1)S(1)}, bf16[2,256,512]{2,1,0:T(8,128)(2,1)S(1)}, u32[]{:S(2)}, u32[]{:S(2)}) collective-permute-start(bf16[2,256,512]{2,1,0:T(8,128)(2,1)S(1)} %bitcast.139), channel_id=1, source_target_pairs={{0,32},{4,36},{8,40},{12,44},{16,48},{20,52},{24,56},{28,60},{32,0... | collective-permute-start | bytes 1572872 | tf_op jit(solution)/shard_map/ppermute | solution.py:10
  17.3 20.6 %collective-permute-start.4 = (bf16[2,256,512]{2,1,0:T(8,128)(2,1)S(1)}, bf16[2,256,512]{2,1,0:T(8,128)(2,1)S(1)}, u32[]{:S(2)}, u32[]{:S(2)}) collective-permute-start(bf16[2,256,512]{2,1,0:T(8,128)(2,1)S(1)} %bitcast.140), channel_id=1, source_target_pairs={{0,64},{4,68},{8,72},{12,76},{16,80},{20,84},{24,88},{28,92},{32,9... | collective-permute-start | bytes 1572872 | tf_op jit(solution)/shard_map/ppermute | solution.py:10
  21.5 19.5 %collective-permute-start.5 = (bf16[2,256,512]{2,1,0:T(8,128)(2,1)S(1)}, bf16[2,256,512]{2,1,0:T(8,128)(2,1)S(1)}, u32[]{:S(2)}, u32[]{:S(2)}) collective-permute-start(bf16[2,256,512]{2,1,0:T(8,128)(2,1)S(1)} %bitcast.142), channel_id=1, source_target_pairs={{0,128},{4,132},{8,136},{12,140},{16,144},{20,148},{24,152},{28,15... | collective-permute-start | bytes 1572872 | tf_op jit(solution)/shard_map/ppermute | solution.py:10
  49.8 9.1 %copy-start = (bf16[256,1024]{1,0:T(8,128)(2,1)S(1)}, bf16[256,1024]{1,0:T(8,128)(2,1)}, u32[]{:S(2)}) copy-start(bf16[256,1024]{1,0:T(8,128)(2,1)} %param.5) | copy-start | bytes 1572868
  49.8 157.6 %all-to-all-start = ((bf16[2,8,256,512]{2,1,0,3:T(8,128)(2,1)}), bf16[2,8,256,512]{2,1,0,3:T(8,128)(2,1)}, u32[]{:S(2)}, u32[]{:S(2)}) async-start(bf16[2,8,256,512]{2,1,0,3:T(8,128)(2,1)} %copy.63), calls=%async_computation | async-start | bytes 8388608 | tf_op jit(solution)/shard_map/all_to_all | solution.py:55
  58.9 163.7 %all-gather.2.cloned.1.call-start = ((), (), s32[]{:S(2)}) async-start(), calls=%async_computation.1 | async-start | bytes 2621440 | tf_op jit(solution)/shard_map/all_gather | solution.py:59
  66.2 13.8 %collective-permute-start.10 = (bf16[2,256,512]{1,2,0:T(8,128)(2,1)S(1)}, bf16[2,256,512]{1,2,0:T(8,128)(2,1)S(1)}, u32[]{:S(2)}, u32[]{:S(2)}) collective-permute-start(bf16[2,256,512]{1,2,0:T(8,128)(2,1)S(1)} %get-tuple-element.18), channel_id=1, source_target_pairs={{0,64},{4,68},{8,72},{12,76},{16,80},{20,84},{24,88},{28,92},{32,9... | collective-permute-start | bytes 1572872 | tf_op jit(solution)/shard_map/ppermute | solution.py:10
  67.4 24.8 %collective-permute-start.11 = (bf16[2,256,512]{1,2,0:T(8,128)(2,1)S(1)}, bf16[2,256,512]{1,2,0:T(8,128)(2,1)S(1)}, u32[]{:S(2)}, u32[]{:S(2)}) collective-permute-start(bf16[2,256,512]{1,2,0:T(8,128)(2,1)S(1)} %get-tuple-element.17), channel_id=1, source_target_pairs={{0,128},{4,132},{8,136},{12,140},{16,144},{20,148},{24,152},{28,15... | collective-permute-start | bytes 1572872 | tf_op jit(solution)/shard_map/ppermute | solution.py:10
  68.7 23.4 %collective-permute-start.6 = (bf16[2,256,512]{1,2,0:T(8,128)(2,1)S(1)}, bf16[2,256,512]{1,2,0:T(8,128)(2,1)S(1)}, u32[]{:S(2)}, u32[]{:S(2)}) collective-permute-start(bf16[2,256,512]{1,2,0:T(8,128)(2,1)S(1)} %get-tuple-element.16), channel_id=1, source_target_pairs={{0,4},{4,0},{8,12},{12,8},{16,20},{20,16},{24,28},{28,24},{32,36},... | collective-permute-start | bytes 1572872 | tf_op jit(solution)/shard_map/ppermute | solution.py:10
  68.7 23.9 %collective-permute-start.7 = (bf16[2,256,512]{1,2,0:T(8,128)(2,1)S(1)}, bf16[2,256,512]{1,2,0:T(8,128)(2,1)S(1)}, u32[]{:S(2)}, u32[]{:S(2)}) collective-permute-start(bf16[2,256,512]{1,2,0:T(8,128)(2,1)S(1)} %get-tuple-element.15), channel_id=1, source_target_pairs={{0,8},{4,12},{8,0},{12,4},{16,24},{20,28},{24,16},{28,20},{32,40},... | collective-permute-start | bytes 1572872 | tf_op jit(solution)/shard_map/ppermute | solution.py:10
  69.8 125.4 %collective-permute-start.8 = (bf16[2,256,512]{1,2,0:T(8,128)(2,1)S(1)}, bf16[2,256,512]{1,2,0:T(8,128)(2,1)S(1)}, u32[]{:S(2)}, u32[]{:S(2)}) collective-permute-start(bf16[2,256,512]{1,2,0:T(8,128)(2,1)S(1)} %get-tuple-element.14), channel_id=1, source_target_pairs={{0,16},{4,20},{8,24},{12,28},{16,0},{20,4},{24,8},{28,12},{32,48},... | collective-permute-start | bytes 1572872 | tf_op jit(solution)/shard_map/ppermute | solution.py:10
  80.0 117.7 %collective-permute-start.9 = (bf16[2,256,512]{1,2,0:T(8,128)(2,1)S(1)}, bf16[2,256,512]{1,2,0:T(8,128)(2,1)S(1)}, u32[]{:S(2)}, u32[]{:S(2)}) collective-permute-start(bf16[2,256,512]{1,2,0:T(8,128)(2,1)S(1)} %get-tuple-element.13), channel_id=1, source_target_pairs={{0,32},{4,36},{8,40},{12,44},{16,48},{20,52},{24,56},{28,60},{32,0... | collective-permute-start | bytes 1572872 | tf_op jit(solution)/shard_map/ppermute | solution.py:10
Sparse Core Ops, SparseCore 0:
  62.1 58.6 all-gather.1
where the time goes:
time: 236 us
  waiting for transfers between devices  143 us (61%)
  local copies, waits for them, and re-layouts  34.9 us (15%)
  starting transfers between devices  24.2 us (10%)
  matrix products  19.3 us (8%)
  between operations  14.1 us (6%)
    ppermute x12, waiting for transfers between devices, partner(): return lax.ppermute(value, axis, pairs)  143 us
    ppermute x12, starting transfers between devices, partner(): return lax.ppermute(value, axis, pairs)  15.2 us
    all_to_all x2, local copies, waits for them, and re-layouts, body(): lax.all_to_all(forward_stack, 'dp', split_axis=3, concat_axis=2, tiled=True)  15.1 us
    unnamed x14, local copies, waits for them, and re-layouts  9.61 us
    all_to_all x1, starting transfers between devices, body(): lax.all_to_all(forward_stack, 'dp', split_axis=3, concat_axis=2, tiled=True)  9.09 us
    another operation x2, local copies, waits for them, and re-layouts, body(): jnp.stack([features] + [partner_rows[level] for level in range(levels)],...  8.75 us
    dot_general x1, matrix products, body(): jnp.einsum('rsta,rsab->rtb', forward_stack, weights, preferred_element_ty...  6.98 us
    dot_general x1, matrix products, body(): jnp.einsum('rsta,rtb->rsab', columns, lax.all_gather(upstream, 'dp', axis...  6.52 us
  transfers between devices with their start and end apart: 14, of which 9 were waited for; matrix products, arithmetic and copies ran while one was open for 13% of the time, Pallas kernels for 0%

commit v1 on v0

--- a/solution.py
+++ b/solution.py
@@ -52,7 +52,12 @@
     input_grad = jnp.transpose(grad_total.astype(jnp.bfloat16), (1, 0, 2)).reshape(
         tokens, row_count * block_size
     )
-    columns = lax.all_to_all(forward_stack, "dp", split_axis=3, concat_axis=2, tiled=True)
+    columns = jnp.concatenate(
+        lax.all_to_all(
+            jnp.stack(jnp.split(forward_stack, lax.axis_size("dp"), axis=3)), "dp", 0, 0
+        ),
+        axis=2,
+    )
     weight_sum = jnp.einsum(
         "rsta,rtb->rsab",
         columns,

time: 236 us -> 225 us (0.953)
  local copies, waits for them, and re-layouts: 34.9 us -> 13.8 us
  starting transfers between devices: 24.2 us -> 28.8 us
  other arithmetic: 0.59 us -> 4.87 us
  waiting for transfers between devices: 143 us -> 140 us
  matrix products: 19.3 us -> 22.1 us
    all_to_all x2 -> x0, local copies, waits for them, and re-layouts: 15.1 us -> none  [body(): lax.all_to_all(forward_stack, 'dp', split_axis=3, concat_axis=2, tiled=True)]
    another operation x2 -> x1, local copies, waits for them, and re-layouts: 8.75 us -> 0.04 us  [body(): jnp.stack([features] + [partner_rows[level] for level in range(levels)],...]
    reshape x0 -> x1, local copies, waits for them, and re-layouts: none -> 4.62 us  [body(): jnp.concatenate(lax.all_to_all(jnp.stack(jnp.split(forward_stack, lax.axi...]
    unnamed x14 -> x20, local copies, waits for them, and re-layouts: 9.61 us -> 5.57 us
    ppermute x12, starting transfers between devices: 15.2 us -> 18.5 us  [partner(): return lax.ppermute(value, axis, pairs)]
    dot_general x1, matrix products: 5.81 us -> 9.06 us  [body(): jnp.einsum('rtb,rsab->rsta', upstream, weights, preferred_element_type=jn...]
    ppermute x12, waiting for transfers between devices: 143 us -> 140 us  [partner(): return lax.ppermute(value, axis, pairs)]
  transfers between devices with their start and end apart: 14 -> 14, of which waited for: 9 -> 5; matrix products, arithmetic and copies ran while one was open for 13% -> 13% of each run, Pallas kernels for 0% -> 0%
where the time goes in v1:
time: 225 us; the launch traced here: 224 us
  waiting for transfers between devices  140 us (62%)
  starting transfers between devices  28.8 us (13%)
  matrix products  22.1 us (10%)
  between operations  14.2 us (6%)
  local copies, waits for them, and re-layouts  13.8 us (6%)
  other arithmetic  4.87 us (2%)
    ppermute x12, waiting for transfers between devices, partner(): return lax.ppermute(value, axis, pairs)  140 us
    ppermute x12, starting transfers between devices, partner(): return lax.ppermute(value, axis, pairs)  18.5 us
    all_to_all x1, starting transfers between devices, body(): lax.all_to_all(jnp.stack(jnp.split(forward_stack, lax.axis_size('dp'), ax...  10.3 us
    dot_general x1, matrix products, body(): jnp.einsum('rtb,rsab->rsta', upstream, weights, preferred_element_type=jn...  9.06 us
    dot_general x1, matrix products, body(): jnp.einsum('rsta,rtb->rsab', columns, lax.all_gather(upstream, 'dp', axis...  6.56 us
    dot_general x1, matrix products, body(): jnp.einsum('rsta,rsab->rtb', forward_stack, weights, preferred_element_ty...  6.51 us
    unnamed x20, local copies, waits for them, and re-layouts  5.57 us
    reshape x1, local copies, waits for them, and re-layouts, body(): jnp.concatenate(lax.all_to_all(jnp.stack(jnp.split(forward_stack, lax.axi...  4.62 us
  transfers between devices with their start and end apart: 14, of which 5 were waited for; matrix products, arithmetic and copies ran while one was open for 13% of the time, Pallas kernels for 0%

profile of v1, /device:TPU:3, one launch (start us, length us, event | category | flops | bytes accessed | tf_op | source)
XLA Modules:
  0.0 223.6 jit_solution(12924438052074654299)
XLA Ops:
  7.2 1.2 copy.21
  8.4 0.2 copy.22
  8.6 1.4 collective-permute-start
  10.0 0.3 collective-permute-start.4
  10.3 3.0 %collective-permute-start.3 = (bf16[2,256,512]{2,1,0:T(8,128)(2,1)S(1)}, bf16[2,256,512]{2,1,0:T(8,128)(2,1)S(1)}, u32[]{:S(2)}, u32[]{:S(2)}) collective-permute-start(bf16[2,256,512]{2,1,0:T(8,128)(2,1)S(1)} %bitcast.141), channel_id=1, source_target_pairs={{0,32},{4,36},{8,40},{12,44},{16,48},{20,52},{24,56},{28,60},{32,0... | collective-permute-start | bytes 1572872 | tf_op jit(solution)/shard_map/ppermute | solution.py:10
  13.3 1.6 collective-permute-start.2
  14.9 2.6 %collective-permute-start.1 = (bf16[2,256,512]{2,1,0:T(8,128)(2,1)S(1)}, bf16[2,256,512]{2,1,0:T(8,128)(2,1)S(1)}, u32[]{:S(2)}, u32[]{:S(2)}) collective-permute-start(bf16[2,256,512]{2,1,0:T(8,128)(2,1)S(1)} %bitcast.143), channel_id=1, source_target_pairs={{0,8},{4,12},{8,0},{12,4},{16,24},{20,28},{24,16},{28,20},{32,40},... | collective-permute-start | bytes 1572872 | tf_op jit(solution)/shard_map/ppermute | solution.py:10
  17.6 3.9 %collective-permute-done = bf16[2,256,512]{2,1,0:T(8,128)(2,1)S(1)} collective-permute-done((bf16[2,256,512]{2,1,0:T(8,128)(2,1)S(1)}, bf16[2,256,512]{2,1,0:T(8,128)(2,1)S(1)}, u32[]{:S(2)}, u32[]{:S(2)}) %collective-permute-start) | collective-permute-done | bytes 524320 | tf_op jit(solution)/shard_map/ppermute | solution.py:10
  21.5 1.8 collective-permute-start.5
  23.4 11.8 %collective-permute-done.1 = bf16[2,256,512]{2,1,0:T(8,128)(2,1)S(1)} collective-permute-done((bf16[2,256,512]{2,1,0:T(8,128)(2,1)S(1)}, bf16[2,256,512]{2,1,0:T(8,128)(2,1)S(1)}, u32[]{:S(2)}, u32[]{:S(2)}) %collective-permute-start.1) | collective-permute-done | bytes 524320 | tf_op jit(solution)/shard_map/ppermute | solution.py:10
  35.2 0.0 collective-permute-done.2
  35.3 0.3 collective-permute-done.3
  35.6 0.0 collective-permute-done.4
  35.7 0.0 collective-permute-done.5
  35.7 0.0 copy-start
  35.7 1.2 slice_bitcast_fusion.3
  36.9 0.8 copy-done
  37.6 2.2 pad_maximum_fusion
  39.9 10.3 %all-to-all-start = ((bf16[4,2,8,256,128]{4,3,2,1,0:T(8,128)(2,1)}), bf16[4,2,8,256,128]{4,3,2,1,0:T(8,128)(2,1)}, u32[]{:S(2)}, u32[]{:S(2)}) async-start(bf16[4,2,8,256,128]{4,3,2,1,0:T(8,128)(2,1)} %pad_maximum_fusion), calls=%async_computation | async-start | bytes 8388608 | tf_op jit(solution)/shard_map/all_to_all | solution.py:56
  50.1 0.0 all-gather.2.cloned.1.call-start
  50.1 0.0 copy-done.3
  50.1 0.2 copy.31
  50.3 1.0 copy.32
  51.4 0.0 all-gather.2.cloned.1.call-update
  51.4 9.1 %fusion.17 = (bf16[2,8,256,512]{2,3,1,0:T(8,128)(2,1)S(1)}, f32[2,8,256,512]{2,3,1,0:T(8,128)}) fusion(bf16[2,8,512,512]{3,2,1,0:T(8,128)(2,1)} %param.4, bf16[256,2,512]{2,0,1:T(8,128)(2,1)} %copy.32), kind=kOutput, calls=%fused_computation.38 | convolution fusion | flops 2149580800 | bytes 21495808 | tf_op jit(solution)/shard_map/rtb,rsab->rsta/dot_general | solution.py:42
  60.4 1.0 slice_bitcast_fusion.11
  61.5 1.2 collective-permute-start.9
  62.7 0.7 collective-permute-start.8
  63.4 2.9 %collective-permute-start.7 = (bf16[2,256,512]{1,2,0:T(8,128)(2,1)S(1)}, bf16[2,256,512]{1,2,0:T(8,128)(2,1)}, u32[]{:S(2)}, u32[]{:S(2)}) collective-permute-start(bf16[2,256,512]{1,2,0:T(8,128)(2,1)S(1)} %get-tuple-element.16), channel_id=1, source_target_pairs={{0,8},{4,12},{8,0},{12,4},{16,24},{20,28},{24,16},{28,20},{32,40},... | collective-permute-start | bytes 1572872 | tf_op jit(solution)/shard_map/ppermute | solution.py:10
  66.3 0.4 collective-permute-start.6
  66.7 1.8 collective-permute-start.11
  68.6 120.1 %collective-permute-done.9 = bf16[2,256,512]{1,2,0:T(8,128)(2,1)S(1)} collective-permute-done((bf16[2,256,512]{1,2,0:T(8,128)(2,1)S(1)}, bf16[2,256,512]{1,2,0:T(8,128)(2,1)S(1)}, u32[]{:S(2)}, u32[]{:S(2)}) %collective-permute-start.9) | collective-permute-done | bytes 524320 | tf_op jit(solution)/shard_map/ppermute | solution.py:10
  188.7 0.7 collective-permute-start.10
  189.4 0.1 copy-done.2
  189.5 0.0 copy-done.1
  189.5 6.5 %fusion.6 = bf16[256,2,512]{2,0,1:T(8,128)(2,1)} fusion(bf16[2,8,256,512]{3,2,1,0:T(8,128)(2,1)S(1)} %copy-done.1, bf16[2,8,512,512]{3,2,1,0:T(8,128)(2,1)} %param.4), kind=kOutput, calls=%fused_computation.7 | convolution fusion | flops 2147745792 | bytes 13107200 | tf_op jit(solution)/shard_map/rsta,rsab->rtb/dot_general | solution.py:36
  196.0 1.2 copy.30
  197.3 1.0 copy.42
  198.3 0.0 collective-permute-done.8
  198.3 0.0 collective-permute-done.7
  198.3 0.0 collective-permute-done.6
  198.3 0.0 collective-permute-done.11
  198.3 3.6 %collective-permute-done.10 = bf16[2,256,512]{1,2,0:T(8,128)(2,1)} collective-permute-done((bf16[2,256,512]{1,2,0:T(8,128)(2,1)S(1)}, bf16[2,256,512]{1,2,0:T(8,128)(2,1)}, u32[]{:S(2)}, u32[]{:S(2)}) %collective-permute-start.10) | collective-permute-done | bytes 524320 | tf_op jit(solution)/shard_map/ppermute | solution.py:10
  201.9 2.6 %fusion.15 = bf16[2,256,512]{1,2,0:T(8,128)(2,1)S(1)} fusion(f32[2,8,256,512]{2,3,1,0:T(8,128)} %get-tuple-element.21, bf16[2,256,512]{1,2,0:T(8,128)(2,1)} %collective-permute-done.11, bf16[2,256,512]{1,2,0:T(8,128)(2,1)} %collective-permute-done.10, bf16[2,256,512]{1,2,0:T(8,128)(2,1)} %copy-done.2, bf16[2,256,512]{1,2,0:T(8,128)(2,1)} %collective-permute-done.8, ...), kind=kLoop, calls=%fused_computation.21 | loop fusion | flops 3932160 | bytes 5242880 | tf_op jit(solution)/shard_map/convert_element_type | solution.py:52
  204.5 1.0 copy.43
  205.5 0.0 all-to-all-done
  205.5 4.6 %copy.40 = bf16[2,8,4,256,128]{4,3,2,1,0:T(8,128)(2,1)} copy(bf16[2,8,4,256,128]{4,3,1,0,2:T(8,128)(2,1)} %bitcast.39) | data formatting | bytes 8388608 | tf_op jit(solution)/shard_map/reshape | solution.py:55
  210.2 6.6 %fusion.2 = bf16[2,8,128,512]{3,2,1,0:T(8,128)(2,1)} fusion(bf16[2,8,1024,128]{3,2,1,0:T(8,128)(2,1)} %bitcast.147, bf16[2,1024,512]{2,1,0:T(8,128)(2,1)} %all-gather.2.cloned.1.call-done), kind=kOutput, calls=%fused_computation.4 | convolution fusion | flops 2148532224 | bytes 8388608 | tf_op jit(solution)/shard_map/rsta,rtb->rsab/dot_general | solution.py:61
  (12 shorter events, 0.3 us)
Async XLA Ops:
  8.6 12.9 %collective-permute-start = (bf16[2,256,512]{2,1,0:T(8,128)(2,1)S(1)}, bf16[2,256,512]{2,1,0:T(8,128)(2,1)S(1)}, u32[]{:S(2)}, u32[]{:S(2)}) collective-permute-start(bf16[2,256,512]{2,1,0:T(8,128)(2,1)S(1)} %bitcast.139), channel_id=1, source_target_pairs={{0,4},{4,0},{8,12},{12,8},{16,20},{20,16},{24,28},{28,24},{32,36},... | collective-permute-start | bytes 1572872 | tf_op jit(solution)/shard_map/ppermute | solution.py:10
  10.0 25.6 %collective-permute-start.4 = (bf16[2,256,512]{2,1,0:T(8,128)(2,1)S(1)}, bf16[2,256,512]{2,1,0:T(8,128)(2,1)S(1)}, u32[]{:S(2)}, u32[]{:S(2)}) collective-permute-start(bf16[2,256,512]{2,1,0:T(8,128)(2,1)S(1)} %bitcast.140), channel_id=1, source_target_pairs={{0,64},{4,68},{8,72},{12,76},{16,80},{20,84},{24,88},{28,92},{32,9... | collective-permute-start | bytes 1572872 | tf_op jit(solution)/shard_map/ppermute | solution.py:10
  10.3 25.3 %collective-permute-start.3 = (bf16[2,256,512]{2,1,0:T(8,128)(2,1)S(1)}, bf16[2,256,512]{2,1,0:T(8,128)(2,1)S(1)}, u32[]{:S(2)}, u32[]{:S(2)}) collective-permute-start(bf16[2,256,512]{2,1,0:T(8,128)(2,1)S(1)} %bitcast.141), channel_id=1, source_target_pairs={{0,32},{4,36},{8,40},{12,44},{16,48},{20,52},{24,56},{28,60},{32,0... | collective-permute-start | bytes 1572872 | tf_op jit(solution)/shard_map/ppermute | solution.py:10
  13.3 22.0 %collective-permute-start.2 = (bf16[2,256,512]{2,1,0:T(8,128)(2,1)S(1)}, bf16[2,256,512]{2,1,0:T(8,128)(2,1)S(1)}, u32[]{:S(2)}, u32[]{:S(2)}) collective-permute-start(bf16[2,256,512]{2,1,0:T(8,128)(2,1)S(1)} %bitcast.142), channel_id=1, source_target_pairs={{0,16},{4,20},{8,24},{12,28},{16,0},{20,4},{24,8},{28,12},{32,48},... | collective-permute-start | bytes 1572872 | tf_op jit(solution)/shard_map/ppermute | solution.py:10
  14.9 20.3 %collective-permute-start.1 = (bf16[2,256,512]{2,1,0:T(8,128)(2,1)S(1)}, bf16[2,256,512]{2,1,0:T(8,128)(2,1)S(1)}, u32[]{:S(2)}, u32[]{:S(2)}) collective-permute-start(bf16[2,256,512]{2,1,0:T(8,128)(2,1)S(1)} %bitcast.143), channel_id=1, source_target_pairs={{0,8},{4,12},{8,0},{12,4},{16,24},{20,28},{24,16},{28,20},{32,40},... | collective-permute-start | bytes 1572872 | tf_op jit(solution)/shard_map/ppermute | solution.py:10
  21.5 14.1 %collective-permute-start.5 = (bf16[2,256,512]{2,1,0:T(8,128)(2,1)S(1)}, bf16[2,256,512]{2,1,0:T(8,128)(2,1)S(1)}, u32[]{:S(2)}, u32[]{:S(2)}) collective-permute-start(bf16[2,256,512]{2,1,0:T(8,128)(2,1)S(1)} %bitcast.145), channel_id=1, source_target_pairs={{0,128},{4,132},{8,136},{12,140},{16,144},{20,148},{24,152},{28,15... | collective-permute-start | bytes 1572872 | tf_op jit(solution)/shard_map/ppermute | solution.py:10
  35.7 1.9 copy-start
  39.9 10.3 %copy-start.3 = (bf16[256,1024]{1,0:T(8,128)(2,1)S(1)}, bf16[256,1024]{1,0:T(8,128)(2,1)}, u32[]{:S(2)}) copy-start(bf16[256,1024]{1,0:T(8,128)(2,1)} %param.5) | copy-start | bytes 1572868
  39.9 165.7 %all-to-all-start = ((bf16[4,2,8,256,128]{4,3,2,1,0:T(8,128)(2,1)}), bf16[4,2,8,256,128]{4,3,2,1,0:T(8,128)(2,1)}, u32[]{:S(2)}, u32[]{:S(2)}) async-start(bf16[4,2,8,256,128]{4,3,2,1,0:T(8,128)(2,1)} %pad_maximum_fusion), calls=%async_computation | async-start | bytes 8388608 | tf_op jit(solution)/shard_map/all_to_all | solution.py:56
  50.1 160.0 %all-gather.2.cloned.1.call-start = ((), (), s32[]{:S(2)}) async-start(), calls=%async_computation.1 | async-start | bytes 2621440 | tf_op jit(solution)/shard_map/all_gather | solution.py:64
  60.4 129.1 %copy-start.1 = (bf16[2,8,256,512]{3,2,1,0:T(8,128)(2,1)S(1)}, bf16[2,8,256,512]{3,2,1,0:T(8,128)(2,1)}, u32[]{:S(2)}) copy-start(bf16[2,8,256,512]{3,2,1,0:T(8,128)(2,1)} %copy-done) | copy-start | bytes 12582916
  61.5 127.2 %collective-permute-start.9 = (bf16[2,256,512]{1,2,0:T(8,128)(2,1)S(1)}, bf16[2,256,512]{1,2,0:T(8,128)(2,1)S(1)}, u32[]{:S(2)}, u32[]{:S(2)}) collective-permute-start(bf16[2,256,512]{1,2,0:T(8,128)(2,1)S(1)} %get-tuple-element.14), channel_id=1, source_target_pairs={{0,32},{4,36},{8,40},{12,44},{16,48},{20,52},{24,56},{28,60},{32,0... | collective-permute-start | bytes 1572872 | tf_op jit(solution)/shard_map/ppermute | solution.py:10
  62.7 135.6 %collective-permute-start.8 = (bf16[2,256,512]{1,2,0:T(8,128)(2,1)}, bf16[2,256,512]{1,2,0:T(8,128)(2,1)}, u32[]{:S(2)}, u32[]{:S(2)}) collective-permute-start(bf16[2,256,512]{1,2,0:T(8,128)(2,1)} %get-tuple-element.15), channel_id=1, source_target_pairs={{0,16},{4,20},{8,24},{12,28},{16,0},{20,4},{24,8},{28,12},{32,48},... | collective-permute-start | bytes 1572872 | tf_op jit(solution)/shard_map/ppermute | solution.py:10
  63.4 134.9 %collective-permute-start.7 = (bf16[2,256,512]{1,2,0:T(8,128)(2,1)S(1)}, bf16[2,256,512]{1,2,0:T(8,128)(2,1)}, u32[]{:S(2)}, u32[]{:S(2)}) collective-permute-start(bf16[2,256,512]{1,2,0:T(8,128)(2,1)S(1)} %get-tuple-element.16), channel_id=1, source_target_pairs={{0,8},{4,12},{8,0},{12,4},{16,24},{20,28},{24,16},{28,20},{32,40},... | collective-permute-start | bytes 1572872 | tf_op jit(solution)/shard_map/ppermute | solution.py:10
  66.3 131.9 %collective-permute-start.6 = (bf16[2,256,512]{1,2,0:T(8,128)(2,1)S(1)}, bf16[2,256,512]{1,2,0:T(8,128)(2,1)}, u32[]{:S(2)}, u32[]{:S(2)}) collective-permute-start(bf16[2,256,512]{1,2,0:T(8,128)(2,1)S(1)} %get-tuple-element.17), channel_id=1, source_target_pairs={{0,4},{4,0},{8,12},{12,8},{16,20},{20,16},{24,28},{28,24},{32,36},... | collective-permute-start | bytes 1572872 | tf_op jit(solution)/shard_map/ppermute | solution.py:10
  66.7 131.5 %collective-permute-start.11 = (bf16[2,256,512]{1,2,0:T(8,128)(2,1)S(1)}, bf16[2,256,512]{1,2,0:T(8,128)(2,1)}, u32[]{:S(2)}, u32[]{:S(2)}) collective-permute-start(bf16[2,256,512]{1,2,0:T(8,128)(2,1)S(1)} %get-tuple-element.18), channel_id=1, source_target_pairs={{0,128},{4,132},{8,136},{12,140},{16,144},{20,148},{24,152},{28,15... | collective-permute-start | bytes 1572872 | tf_op jit(solution)/shard_map/ppermute | solution.py:10
  188.7 0.8 copy-start.2
  188.7 13.2 %collective-permute-start.10 = (bf16[2,256,512]{1,2,0:T(8,128)(2,1)S(1)}, bf16[2,256,512]{1,2,0:T(8,128)(2,1)}, u32[]{:S(2)}, u32[]{:S(2)}) collective-permute-start(bf16[2,256,512]{1,2,0:T(8,128)(2,1)S(1)} %get-tuple-element.19), channel_id=1, source_target_pairs={{0,64},{4,68},{8,72},{12,76},{16,80},{20,84},{24,88},{28,92},{32,9... | collective-permute-start | bytes 1572872 | tf_op jit(solution)/shard_map/ppermute | solution.py:10
Sparse Core Ops, SparseCore 0:
  53.3 54.2 all-gather.1
